TPU v7x, 32 devices: a whole 2x2x4 slice. The times are simulated.
32 devices in a mesh: groups: 2 (over x), seq: 16 (over z, y, core).
Axes of the slice: x: 2, y: 2, z: 4, core: 2. Of those that a mesh axis runs over, the one named last changes fastest.
Arguments:
- hidden_in: bfloat16 [16384, 768], P(('groups', 'seq')), parts along dimension 0
- ln_gain: float32 [2, 768], replicated, may hold values from 0.5 to 1.5
- w_qkv: bfloat16 [2, 768, 2304], replicated
- w_out: bfloat16 [2, 768, 768], replicated, may hold values from -0.21875 to 0.21875
- final_gain: float32 [768], replicated, may hold values from 0.5 to 1.5
- w_heads: bfloat16 [768, 512], replicated
- actions: int32 [16384], P(('groups', 'seq')), parts along dimension 0, may hold values from 0 to 255
- propensity: int32 [16384], P(('groups', 'seq')), parts along dimension 0, may hold values from 1024 to 65535
- logged_reward: float32 [16384], P(('groups', 'seq')), parts along dimension 0, may hold values from -6 to 6
- switch_index: int32 [2], P('groups'), parts along dimension 0, may hold values from 2 to 9
Outputs:
- rewards: float32 [16384], P(('groups', 'seq')), parts along dimension 0
- dr_terms: float32 [16384], P(('groups', 'seq')), parts along dimension 0
There are 2 independent parts, one for each index of `groups`. A program takes and returns all parts, laid end to end along the dimension named above; an argument that names none is the same for every part. Nothing has to cross between parts.
All inputs are finite; a program needn't handle non-finite values.
Results may differ from a plain program's by a relative error of at most 0.03.
Values may be sent and summed in bfloat16 or wider, within the bound.
A program may use at most 128 MiB of HBM per device.

v0:
```python
import jax
import jax.numpy as jnp
from jax import lax
from jax.sharding import PartitionSpec as P

HEADS = 12
HEAD = 64
HALF = 256
PROMPT = 256
ACTIONS = 256
LAYERS = 2


def with_halo(array, sides, width):
    for axis, dim in sides:
        count, length = (lax.axis_size(axis), array.shape[dim])
        up = [(i, (i + 1) % count) for i in range(count - 1)]
        down = [(j, i) for i, j in up]
        last = lax.slice_in_dim(array, length - width, length, axis=dim)
        leading = lax.slice_in_dim(array, 0, width, axis=dim)
        before = lax.ppermute(last, axis, up)
        after = lax.ppermute(leading, axis, down)
        array = jnp.concatenate([before, array, after], axis=dim)
    return array


def spread(block, axis, source):
    block = jnp.where(lax.axis_index(axis) == source, block, jnp.zeros_like(block))
    return lax.psum(block, axis)


def layer_norm(hidden_state, gain_row):
    values_f = hidden_state.astype(jnp.float32)
    row_mean = jnp.mean(values_f, axis=-1, keepdims=True)
    centred = values_f - row_mean
    row_var = jnp.mean(centred * centred, axis=-1, keepdims=True)
    return (centred * lax.rsqrt(row_var + 1e-05) * gain_row).astype(jnp.bfloat16)


def attend_block(
    query_block, key_block, value_block, prompt_keys, prompt_values, row_start, total_len
):
    block_rows = query_block.shape[0]
    band_width = key_block.shape[0]
    band_scores = jnp.einsum(
        "qhe,khe->hqk", query_block, key_block, preferred_element_type=jnp.float32
    )
    prompt_scores = jnp.einsum(
        "qhe,khe->hqk", query_block, prompt_keys, preferred_element_type=jnp.float32
    )
    query_pos = row_start + jnp.arange(block_rows, dtype=jnp.int32)
    key_pos = row_start - HALF + jnp.arange(band_width, dtype=jnp.int32)
    prompt_pos = jnp.arange(PROMPT, dtype=jnp.int32)
    band_mask = (
        (jnp.abs(key_pos[None, :] - query_pos[:, None]) <= HALF)
        & (key_pos[None, :] >= 0)
        & (key_pos[None, :] < total_len)
    )
    prompt_mask = jnp.abs(prompt_pos[None, :] - query_pos[:, None]) > HALF
    scores = jnp.concatenate(
        [
            jnp.where(prompt_mask[None], prompt_scores, -1e30),
            jnp.where(band_mask[None], band_scores, -1e30),
        ],
        axis=-1,
    )
    row_max = jnp.max(scores, axis=-1, keepdims=True)
    exps = jnp.exp(scores - row_max)
    attn_probs = (exps / jnp.sum(exps, axis=-1, keepdims=True)).astype(jnp.bfloat16)
    value_rows = jnp.concatenate([prompt_values, value_block], axis=0)
    attn_out = jnp.einsum(
        "hqk,khe->qhe", attn_probs, value_rows, preferred_element_type=jnp.float32
    )
    return attn_out.reshape(block_rows, HEADS * HEAD).astype(jnp.bfloat16)


def per_device(
    hidden_in,
    ln_gain,
    w_qkv,
    w_out,
    final_gain,
    w_heads,
    actions,
    propensity,
    logged_reward,
    switch_index,
):
    tok_rows = hidden_in.shape[0]
    feat_width = hidden_in.shape[1]
    seq_devices = lax.axis_size("seq")
    seq_place = lax.axis_index("seq")
    total_len = tok_rows * seq_devices
    first_pos = seq_place * tok_rows
    block_rows = min(256, tok_rows)
    block_count = tok_rows // block_rows
    hidden_state = hidden_in
    for layer_idx in range(LAYERS):
        normed = layer_norm(hidden_state, ln_gain[layer_idx])
        weights = w_qkv[layer_idx]
        projected = jnp.dot(normed, weights, preferred_element_type=jnp.float32)
        queries = (projected[:, :feat_width] * 0.125).astype(jnp.bfloat16)
        key_value = projected[:, feat_width:].astype(jnp.bfloat16)
        extended = with_halo(key_value, (("seq", 0),), HALF)
        prompt_kv = spread(key_value[:PROMPT], "seq", 0)
        query_heads = queries.reshape(tok_rows, HEADS, HEAD)
        band_keys = extended[:, :feat_width].reshape(-1, HEADS, HEAD)
        band_values = extended[:, feat_width:].reshape(-1, HEADS, HEAD)
        prompt_keys = prompt_kv[:, :feat_width].reshape(PROMPT, HEADS, HEAD)
        prompt_values = prompt_kv[:, feat_width:].reshape(PROMPT, HEADS, HEAD)

        def one_block(block_idx):
            local_start = block_idx * block_rows
            return attend_block(
                lax.dynamic_slice_in_dim(query_heads, local_start, block_rows),
                lax.dynamic_slice_in_dim(band_keys, local_start, block_rows + 2 * HALF),
                lax.dynamic_slice_in_dim(band_values, local_start, block_rows + 2 * HALF),
                prompt_keys,
                prompt_values,
                first_pos + local_start,
                total_len,
            )

        attended = lax.map(one_block, jnp.arange(block_count, dtype=jnp.int32)).reshape(
            tok_rows, feat_width
        )
        projection = jnp.dot(attended, w_out[layer_idx], preferred_element_type=jnp.float32)
        hidden_state = (hidden_state.astype(jnp.float32) + projection).astype(jnp.bfloat16)
    final = layer_norm(hidden_state, final_gain)
    head_out = jnp.dot(final, w_heads, preferred_element_type=jnp.float32)
    logits = head_out[:, :ACTIONS]
    reward_table = head_out[:, ACTIONS:]
    logit_max = jnp.max(logits, axis=-1, keepdims=True)
    exps = jnp.exp(logits - logit_max)
    policy = exps / jnp.sum(exps, axis=-1, keepdims=True)
    chosen = actions[:, None] == jnp.arange(ACTIONS, dtype=jnp.int32)[None, :]
    rewards = jnp.sum(jnp.where(chosen, reward_table, 0.0), axis=-1)
    chosen_prob = jnp.sum(jnp.where(chosen, policy, 0.0), axis=-1)
    direct = jnp.sum(policy * reward_table, axis=-1)
    logged_prob = propensity.astype(jnp.float32) / 65536.0
    cutoff = 0.5 * switch_index[0].astype(jnp.float32)
    dr_terms = direct + jnp.minimum(chosen_prob / logged_prob, cutoff) * (logged_reward - rewards)
    return (rewards, dr_terms)


def solution(mesh):
    placed = (
        P(("groups", "seq"), None),
        P(),
        P(),
        P(),
        P(),
        P(),
        P(("groups", "seq")),
        P(("groups", "seq")),
        P(("groups", "seq")),
        P("groups"),
    )
    return jax.shard_map(
        per_device,
        mesh=mesh,
        in_specs=placed,
        out_specs=(P(("groups", "seq")), P(("groups", "seq"))),
        check_vma=False,
    )
```

profile of v0, /device:TPU:20, one launch (start us, length us, event | category | flops | bytes accessed | tf_op | source)
XLA Modules:
  0.0 359.7 jit_solution(2516836620028198546)
XLA Ops:
  8.6 1.5 fusion.55
  11.5 6.5 %fusion.92 = (bf16[512,2304]{1,0:T(8,128)(2,1)S(1)}, f32[512,2304]{1,0:T(8,128)}) fusion(bf16[2,768,2304]{2,1,0:T(8,128)(2,1)} %param.16, bf16[512,768]{1,0:T(8,128)(2,1)} %param.14, f32[768]{0:T(1024)S(1)} %get-tuple-element.252, f32[512]{0:T(512)S(1)} %add_rsqrt_fusion.2, f32[512]{0:T(512)S(1)} %broadcast_multiply_fusion.2), kind=kOutput, calls=%fused_computation.135 | convolution fusion | flops 1815085056 | bytes 11410432 | tf_op jit(solution)/shard_map/dot_general | solution.py:101
  19.4 1.5 broadcast_select_fusion.3
  21.0 1.9 collective-permute-start.1
  22.9 2.4 collective-permute-start
  25.6 1.5 slice.105
  27.1 1.5 fusion.64
  29.8 91.5 %all-reduce.3.cloned.1.call-done = bf16[256,1536]{1,0:T(8,128)(2,1)} async-done(((bf16[256,1536]{1,0:T(8,128)(2,1)}), bf16[256,1536]{1,0:T(8,128)(2,1)}) %all-reduce.3.cloned.1.call-update) | async-done | bytes 786448 | tf_op jit(solution)/shard_map/psum | solution.py:29
  124.3 1.5 pad_maximum_fusion
  125.8 1.9 fusion.89
  127.7 1.7 copy.30
  129.4 2.6 copy.26
  133.5 45.4 %while.24 = (s32[]{:T(128)}, bf16[2,256,768]{2,1,0:T(8,128)(2,1)}, s32[2]{0:T(128)}, bf16[1024,12,64]{0,2,1:T(8,128)(2,1)}, bf16[256,12,64]{0,2,1:T(8,128)(2,1)}...) while((s32[]{:T(128)}, bf16[2,256,768]{2,1,0:T(8,128)(2,1)}, ...), condition=%wide.region_7.8_spmd, body=%wide.region_3.7_spmd.sunk | while | flops 838137088 | bytes 71819664 | solution.py:124
  138.0 2.3 fusion.120
  140.4 3.5 copy.46
  143.9 2.9 fusion.119
  146.8 2.9 fusion.121
  149.7 4.5 %fusion.122 = bf16[12,64,256]{2,1,0:T(8,128)(2,1)} fusion(f32[12,256,768]{2,1,0:T(8,128)S(1)} %get-tuple-element.438, f32[12,256,256]{2,1,0:T(8,128)S(1)} %copy-done.1, f32[12,256]{1,0:T(8,128)S(1)} %fusion.121, f32[12,256]{1,0:T(8,128)S(1)} %reduce_max.69, bf16[768,12,64]{0,2,1:T(8,128)(2,1)S(1)} %constant_dynamic-slice_fusion.4, ...), kind=kOutput, calls=%fused_computation.10.clone.1 | convolution fusion | flops 418578432 | bytes 14573568 | tf_op jit(solution)/shard_map/while/body/eval_jaxpr/hqk,khe->qhe/dot_general | solution.py:71
  160.7 2.4 fusion.120
  163.0 3.5 copy.46
  166.6 3.0 fusion.119
  169.6 2.9 fusion.121
  172.4 4.5 %fusion.122 = bf16[12,64,256]{2,1,0:T(8,128)(2,1)} fusion(f32[12,256,768]{2,1,0:T(8,128)S(1)} %get-tuple-element.438, f32[12,256,256]{2,1,0:T(8,128)S(1)} %copy-done.1, f32[12,256]{1,0:T(8,128)S(1)} %fusion.121, f32[12,256]{1,0:T(8,128)S(1)} %reduce_max.69, bf16[768,12,64]{0,2,1:T(8,128)(2,1)S(1)} %constant_dynamic-slice_fusion.4, ...), kind=kOutput, calls=%fused_computation.10.clone.1 | convolution fusion | flops 418578432 | bytes 14573568 | tf_op jit(solution)/shard_map/while/body/eval_jaxpr/hqk,khe->qhe/dot_general | solution.py:71
  178.9 2.6 convert_reduce_fusion
  181.9 6.3 %fusion.93 = (bf16[512,2304]{1,0:T(8,128)(2,1)S(1)}, f32[512,2304]{1,0:T(8,128)}) fusion(bf16[2,768,2304]{2,1,0:T(8,128)(2,1)} %param.16, bf16[512,768]{1,0:T(8,128)(2,1)S(1)} %get-tuple-element.318, f32[768]{0:T(1024)S(1)} %copy-done.13, f32[512]{0:T(512)S(1)} %add_rsqrt_fusion.1, f32[512]{0:T(512)S(1)} %broadcast_multiply_fusion.1), kind=kOutput, calls=%fused_computation.136 | convolution fusion | flops 1815085056 | bytes 11410432 | tf_op jit(solution)/shard_map/dot_general | solution.py:101
  188.1 1.4 copy-done.7
  189.6 1.5 broadcast_select_fusion.2
  191.1 1.9 collective-permute-start.3
  193.0 2.6 collective-permute-start.2
  196.3 1.5 slice.113
  197.8 1.5 fusion.63
  200.6 90.1 %all-reduce.5.cloned.1.call-done = bf16[256,1536]{1,0:T(8,128)(2,1)} async-done(((bf16[256,1536]{1,0:T(8,128)(2,1)}), bf16[256,1536]{1,0:T(8,128)(2,1)}) %all-reduce.5.cloned.1.call-update) | async-done | bytes 786448 | tf_op jit(solution)/shard_map/psum | solution.py:29
  293.7 1.5 pad_maximum_fusion.1
  295.2 1.9 fusion.88
  297.1 1.7 copy.36
  298.8 2.6 copy.32
  302.8 45.1 %while.25 = (s32[]{:T(128)}, bf16[2,256,768]{2,1,0:T(8,128)(2,1)}, s32[2]{0:T(128)}, bf16[1024,12,64]{0,2,1:T(8,128)(2,1)}, bf16[256,12,64]{0,2,1:T(8,128)(2,1)}...) while((s32[]{:T(128)}, bf16[2,256,768]{2,1,0:T(8,128)(2,1)}, ...), condition=%wide.region_15.16_spmd, body=%wide.region_11.15_spmd.sunk | while | flops 838137088 | bytes 71819664 | solution.py:124
  307.3 2.3 fusion.128
  309.6 3.5 copy.48
  313.1 2.9 fusion.127
  316.1 2.9 fusion.129
  318.9 4.5 %fusion.130 = bf16[12,64,256]{2,1,0:T(8,128)(2,1)} fusion(f32[12,256,768]{2,1,0:T(8,128)S(1)} %get-tuple-element.453, f32[12,256,256]{2,1,0:T(8,128)S(1)} %copy-done.2, f32[12,256]{1,0:T(8,128)S(1)} %fusion.129, f32[12,256]{1,0:T(8,128)S(1)} %reduce_max.72, bf16[768,12,64]{0,2,1:T(8,128)(2,1)S(1)} %constant_dynamic-slice_fusion.5, ...), kind=kOutput, calls=%fused_computation.38.clone.1 | convolution fusion | flops 418578432 | bytes 14573568 | tf_op jit(solution)/shard_map/while/body/eval_jaxpr/hqk,khe->qhe/dot_general | solution.py:71
  329.8 2.3 fusion.128
  332.1 3.5 copy.48
  335.7 3.0 fusion.127
  338.7 2.9 fusion.129
  341.5 4.5 %fusion.130 = bf16[12,64,256]{2,1,0:T(8,128)(2,1)} fusion(f32[12,256,768]{2,1,0:T(8,128)S(1)} %get-tuple-element.453, f32[12,256,256]{2,1,0:T(8,128)S(1)} %copy-done.2, f32[12,256]{1,0:T(8,128)S(1)} %fusion.129, f32[12,256]{1,0:T(8,128)S(1)} %reduce_max.72, bf16[768,12,64]{0,2,1:T(8,128)(2,1)S(1)} %constant_dynamic-slice_fusion.5, ...), kind=kOutput, calls=%fused_computation.38.clone.1 | convolution fusion | flops 418578432 | bytes 14573568 | tf_op jit(solution)/shard_map/while/body/eval_jaxpr/hqk,khe->qhe/dot_general | solution.py:71
  348.0 2.6 convert_reduce_fusion.2
  (126 shorter events, 41.5 us)
Async XLA Ops:
  7.2 343.8 %copy-start = (bf16[768,512]{1,0:T(8,128)(2,1)S(1)}, bf16[768,512]{1,0:T(8,128)(2,1)}, u32[]{:S(2)}) copy-start(bf16[768,512]{1,0:T(8,128)(2,1)} %param.19) | copy-start | bytes 2359300
  7.2 114.1 %all-reduce.3.cloned.1.call-start = ((), (), s32[]{:S(2)}) async-start(), calls=%async_computation | async-start | bytes 1572864 | tf_op jit(solution)/shard_map/psum | solution.py:29
  18.0 1.4 copy-start.8
  21.0 103.3 %collective-permute-start.1 = (bf16[256,1536]{1,0:T(8,128)(2,1)}, bf16[256,1536]{1,0:T(8,128)(2,1)}, u32[]{:S(2)}, u32[]{:S(2)}) collective-permute-start(bf16[256,1536]{1,0:T(8,128)(2,1)} %get-tuple-element.309), channel_id=1, source_target_pairs={{1,0},{2,1},{3,2},{4,3},{5,4},{6,5},{7,6},{8,7},{9,8},{10,9},{11,1... | collective-permute-start | bytes 2359304 | tf_op jit(solution)/shard_map/ppermute | solution.py:22
  22.9 101.4 %collective-permute-start = (bf16[256,1536]{1,0:T(8,128)(2,1)}, bf16[256,1536]{1,0:T(8,128)(2,1)}, u32[]{:S(2)}, u32[]{:S(2)}) collective-permute-start(bf16[256,1536]{1,0:T(8,128)(2,1)} %get-tuple-element.310), channel_id=1, source_target_pairs={{0,1},{1,2},{2,3},{3,4},{4,5},{5,6},{6,7},{7,8},{8,9},{9,10},{10,1... | collective-permute-start | bytes 2359304 | tf_op jit(solution)/shard_map/ppermute | solution.py:21
  25.3 265.4 %all-reduce.5.cloned.1.call-start = ((), (), s32[]{:S(2)}) async-start(), calls=%async_computation.1 | async-start | bytes 1572864 | tf_op jit(solution)/shard_map/psum | solution.py:29
  135.5 2.5 copy-start.4
  135.5 2.5 copy-start.6
  143.9 2.9 copy-start.1
  146.8 2.9 copy-start.11
  158.1 2.5 copy-start.4
  158.1 2.5 copy-start.6
  166.6 3.0 copy-start.1
  169.6 2.9 copy-start.11
  178.9 3.0 copy-start.13
  181.5 6.7 %copy-start.9 = (bf16[512,768]{1,0:T(8,128)(2,1)}, bf16[512,768]{1,0:T(8,128)(2,1)S(1)}, u32[]{:S(2)}) copy-start(bf16[512,768]{1,0:T(8,128)(2,1)S(1)} %get-tuple-element.318) | copy-start | bytes 2359300
  188.1 1.4 copy-start.7
  191.1 102.6 %collective-permute-start.3 = (bf16[256,1536]{1,0:T(8,128)(2,1)}, bf16[256,1536]{1,0:T(8,128)(2,1)}, u32[]{:S(2)}, u32[]{:S(2)}) collective-permute-start(bf16[256,1536]{1,0:T(8,128)(2,1)} %get-tuple-element.306), channel_id=1, source_target_pairs={{1,0},{2,1},{3,2},{4,3},{5,4},{6,5},{7,6},{8,7},{9,8},{10,9},{11,1... | collective-permute-start | bytes 2359304 | tf_op jit(solution)/shard_map/ppermute | solution.py:22
  193.0 100.7 %collective-permute-start.2 = (bf16[256,1536]{1,0:T(8,128)(2,1)}, bf16[256,1536]{1,0:T(8,128)(2,1)}, u32[]{:S(2)}, u32[]{:S(2)}) collective-permute-start(bf16[256,1536]{1,0:T(8,128)(2,1)} %get-tuple-element.307), channel_id=1, source_target_pairs={{0,1},{1,2},{2,3},{3,4},{4,5},{5,6},{6,7},{7,8},{8,9},{9,10},{10,1... | collective-permute-start | bytes 2359304 | tf_op jit(solution)/shard_map/ppermute | solution.py:21
  304.7 2.5 copy-start.3
  304.7 2.5 copy-start.5
  313.1 2.9 copy-start.2
  316.1 2.9 copy-start.10
  327.2 2.5 copy-start.3
  327.3 2.5 copy-start.5
  335.7 3.0 copy-start.2
  338.7 2.9 copy-start.10
  348.0 3.0 copy-start.17
  350.6 1.4 copy-start.14
  351.0 1.2 copy-start.15
  351.0 1.2 copy-start.16
  352.2 0.6 copy-start.12
Sparse Core Ops, SparseCore 0:
  25.5 95.7 all-reduce.2
  195.8 94.8 all-reduce.4
where the time goes:
time: 363 us; the launch traced here: 360 us
  waiting for transfers between devices  182 us (50%)
  local copies, waits for them, and re-layouts  63.7 us (18%)
  matrix products  57.6 us (16%)
  other arithmetic  29.6 us (8%)
  between operations  14.9 us (4%)
  starting transfers between devices  9.11 us (3%)
    psum x2, waiting for transfers between devices, spread(): return lax.psum(block, axis)  182 us
    dot_general x4, matrix products, attend_block(): jnp.einsum('hqk,khe->qhe', attn_probs, value_rows, preferred_element_type...  17.9 us
    select_n x4, local copies, waits for them, and re-layouts, attend_block(): jnp.where(prompt_mask[None], prompt_scores, -1e+30)  14.2 us
    dot_general x2, matrix products, per_device(): projected = jnp.dot(normed, weights, preferred_element_type=jnp.float32)  12.7 us
    dot_general x4, matrix products, attend_block(): jnp.einsum('qhe,khe->hqk', query_block, key_block, preferred_element_type...  11.7 us
    reduce_sum x4, other arithmetic, attend_block(): jnp.sum(exps, axis=-1, keepdims=True)  11.4 us
    dot_general x4, matrix products, attend_block(): jnp.einsum('qhe,khe->hqk', query_block, prompt_keys, preferred_element_ty...  9.38 us
    dynamic_update_slice x8, local copies, waits for them, and re-layouts, per_device(): lax.map(one_block, jnp.arange(block_count, dtype=jnp.int32))  7.84 us
  transfers between devices with their start and end apart: 6, of which 2 were waited for; matrix products, arithmetic and copies ran while one was open for 4% of the time, Pallas kernels for 0%

commit v1 on v0

v1 whole, which is shorter than its diff:
```python
import functools

import jax
import jax.numpy as jnp
from jax import lax
from jax.experimental import pallas as pl
from jax.experimental.pallas import tpu as pltpu
from jax.sharding import PartitionSpec as P

HEADS = 12
HEAD = 64
HALF = 256
PROMPT = 256
ACTIONS = 256
LAYERS = 2
BLOCK = 256
TILE = 256
PAIR = 2 * HEAD
CHUNKS = 4
MESH = pl.DeviceIdType.MESH
AT_PROMPT, AT_BEFORE, AT_OWN = 0, PROMPT, PROMPT + HALF
LOG2E = 1.4426950408889634


def norm_rows(rows, gain_row):
    row_mean = jnp.mean(rows, axis=-1, keepdims=True)
    centred = rows - row_mean
    row_var = jnp.mean(centred * centred, axis=-1, keepdims=True)
    return (centred * lax.rsqrt(row_var + 1e-05) * gain_row).astype(jnp.bfloat16)


def kernel(
    n,
    hidden_ref,
    gain_ref,
    final_gain_ref,
    actions_ref,
    propensity_ref,
    logged_ref,
    switch_ref,
    w_qkv_hbm,
    w_out_hbm,
    w_heads_hbm,
    rewards_ref,
    dr_ref,
    w_qkv,
    w_out,
    w_heads,
    states,
    q_s,
    k_s,
    va_s,
    vb_s,
    att_s,
    h_s,
    bias_s,
    load_sem,
    halo_send,
    halo_recv,
    tree_send,
    tree_recv,
):
    tok_rows, width = hidden_ref.shape
    at_after = AT_OWN + tok_rows
    tiles = width // TILE
    pairs = HEADS // 2
    me = lax.axis_index("seq")
    chip, core = me // 2, me % 2
    depth = chip // 2 + chip % 2 + core
    points = CHUNKS + (n // 2 - 1) // 2 + 2
    parent = jnp.where(core == 1, me - 1, jnp.where(chip % 2 == 1, me - 2, me - 4))
    even = core == 0
    children = (
        (me + 4, even & (chip % 2 == 0) & (me + 4 < n)),
        (me + 2, even & (chip % 2 == 0) & (me + 2 < n)),
        (me + 1, even & (me + 1 < n)),
    )
    has_left, has_right, has_parent = me > 0, me < n - 1, me > 0

    loads = [pltpu.make_async_copy(w_qkv_hbm.at[0], w_qkv.at[0], load_sem.at[0])]
    loads.append(pltpu.make_async_copy(w_out_hbm.at[0], w_out.at[0], load_sem.at[1]))
    loads.append(pltpu.make_async_copy(w_qkv_hbm.at[1], w_qkv.at[1], load_sem.at[2]))
    loads.append(pltpu.make_async_copy(w_out_hbm.at[1], w_out.at[1], load_sem.at[3]))
    loads.append(pltpu.make_async_copy(w_heads_hbm, w_heads, load_sem.at[4]))
    for load in loads:
        load.start()

    barrier = pltpu.get_barrier_semaphore()
    partners = ((me - 1, has_left), (me + 1, has_right), (parent, has_parent)) + children
    for partner, there in partners:

        @pl.when(there)
        def _(partner=partner):
            pl.semaphore_signal(barrier, inc=1, device_id={"seq": partner}, device_id_type=MESH)

    def halo(layer, side):
        src = AT_OWN if side == 0 else at_after - HALF
        dst = at_after if side == 0 else AT_BEFORE
        return pltpu.make_async_remote_copy(
            src_ref=states.at[layer, pl.ds(src, HALF)],
            dst_ref=states.at[layer, pl.ds(dst, HALF)],
            send_sem=halo_send.at[layer, side],
            recv_sem=halo_recv.at[layer, side],
            device_id={"seq": me - 1 if side == 0 else me + 1},
            device_id_type=MESH,
        )

    def piece(layer, chunk, slot, target):
        rows = PROMPT // CHUNKS
        part = states.at[layer, pl.ds(pl.multiple_of(chunk * rows, rows), rows)]
        return pltpu.make_async_remote_copy(
            src_ref=part,
            dst_ref=part,
            send_sem=tree_send.at[layer, slot, chunk],
            recv_sem=tree_recv.at[layer, chunk],
            device_id={"seq": target},
            device_id_type=MESH,
        )

    def pass_on(layer, point):
        chunk = point - depth

        @pl.when((chunk >= 0) & (chunk < CHUNKS))
        def _():
            @pl.when(has_parent)
            def _():
                piece(layer, chunk, 0, parent).wait_recv()

            for slot, (child, there) in enumerate(children):

                @pl.when(there)
                def _(slot=slot, child=child):
                    piece(layer, chunk, slot, child).start()

    def finish_passing(layer, done):
        if done < points:

            @pl.loop(done, points)
            def _(point):
                pass_on(layer, point)

    def wait_halo(layer, side):
        @pl.when(has_right if side == 0 else has_left)
        def _():
            halo(layer, side).wait_recv()

    def send_halo(layer, side):
        @pl.when(has_left if side == 0 else has_right)
        def _():
            halo(layer, side).start()

    def start_prompt(layer):
        @pl.when(me == 0)
        def _():
            states[layer, pl.ds(AT_PROMPT, PROMPT), :] = states[layer, pl.ds(AT_OWN, PROMPT), :]

    lane = lax.broadcasted_iota(jnp.int32, (1, PAIR), 1)
    first_half = lane < HEAD

    def project_kv(layer, row, rows, j):
        x = states[layer, pl.ds(row, rows), :]
        for which in (1, 2):
            at = pl.multiple_of(which * width + j * TILE, TILE)
            out = jnp.dot(x, w_qkv[layer, :, pl.ds(at, TILE)], preferred_element_type=jnp.float32)
            for part in range(TILE // PAIR):
                cols = out[:, part * PAIR : (part + 1) * PAIR]
                slot = j * (TILE // PAIR) + part
                if which == 1:
                    k_s[slot, pl.ds(row, rows), :] = cols.astype(jnp.bfloat16)
                else:
                    va_s[slot, pl.ds(row, rows), :] = jnp.where(first_half, cols, 1.0).astype(
                        jnp.bfloat16
                    )
                    vb_s[slot, pl.ds(row, rows), :] = jnp.where(first_half, 1.0, cols).astype(
                        jnp.bfloat16
                    )

    def project_q(layer, j):
        at = pl.multiple_of(j * TILE, TILE)
        x = states[layer, pl.ds(AT_OWN, tok_rows), :]
        out = jnp.dot(x, w_qkv[layer, :, pl.ds(at, TILE)], preferred_element_type=jnp.float32)
        out = out * (0.125 * LOG2E)
        for part in range(TILE // PAIR):
            cols = out[:, part * PAIR : (part + 1) * PAIR]
            slot = j * (TILE // PAIR) + part
            qa = jnp.where(first_half, cols, 0.0).astype(jnp.bfloat16)
            qb = jnp.where(first_half, 0.0, cols).astype(jnp.bfloat16)
            for block in range(tok_rows // BLOCK):
                rows = slice(block * BLOCK, (block + 1) * BLOCK)
                q_s[slot, block, pl.ds(0, BLOCK), :] = qa[rows]
                q_s[slot, block, pl.ds(BLOCK, BLOCK), :] = qb[rows]

    def attend(layer, block, pair):
        band = AT_BEFORE + block * BLOCK
        starts = (AT_PROMPT, band, band + BLOCK, band + 2 * BLOCK)
        q = q_s[pair, block]
        scores = []
        for which, start in enumerate(starts):
            s = lax.dot_general(
                q,
                k_s[pair, pl.ds(start, BLOCK), :],
                (((1,), (1,)), ((), ())),
                preferred_element_type=jnp.float32,
            )
            if which != 2:
                bias = bias_s[block, min(which, 2)]
                s = jnp.concatenate([s[:BLOCK] + bias, s[BLOCK:] + bias], axis=0)
            scores.append(s)
        top = jnp.maximum(
            jnp.maximum(scores[0], scores[1]), jnp.maximum(scores[2], scores[3])
        )
        top = jnp.max(top, axis=-1, keepdims=True)
        out_a = jnp.zeros((BLOCK, PAIR), jnp.float32)
        out_b = jnp.zeros((BLOCK, PAIR), jnp.float32)
        for s, start in zip(scores, starts):
            p = jnp.exp2(s - top).astype(jnp.bfloat16)
            out_a += jnp.dot(
                p[:BLOCK], va_s[pair, pl.ds(start, BLOCK), :], preferred_element_type=jnp.float32
            )
            out_b += jnp.dot(
                p[BLOCK:], vb_s[pair, pl.ds(start, BLOCK), :], preferred_element_type=jnp.float32
            )
        total = pltpu.roll(jnp.where(first_half, out_b, out_a), HEAD, 1)
        att = jnp.where(first_half, out_a, out_b) / total
        att_s[:, pl.ds(pl.multiple_of(pair * PAIR, PAIR), PAIR)] = att.astype(jnp.bfloat16)

    def add_out(layer, block):
        rows = pl.ds(block * BLOCK, BLOCK)
        source = hidden_ref if layer == 0 else h_s
        old = source[rows, :].astype(jnp.float32)
        new = old + jnp.dot(att_s[...], w_out[layer], preferred_element_type=jnp.float32)
        return new.astype(jnp.bfloat16)

    def head(block, h):
        rows = pl.ds(block * BLOCK, BLOCK)
        final = norm_rows(h.astype(jnp.float32), final_gain_ref[...])
        out = jnp.dot(final, w_heads[...], preferred_element_type=jnp.float32)
        logits, table = out[:, :ACTIONS], out[:, ACTIONS:]
        exps = jnp.exp(logits - jnp.max(logits, axis=-1, keepdims=True))
        norm = jnp.sum(exps, axis=-1, keepdims=True)
        action = jnp.broadcast_to(actions_ref[:, rows].astype(jnp.float32), (128, BLOCK))
        action = jnp.transpose(action)[:, :1].astype(jnp.int32)
        chosen = action == lax.broadcasted_iota(jnp.int32, (1, ACTIONS), 1)
        reward = jnp.sum(jnp.where(chosen, table, 0.0), axis=-1, keepdims=True)
        prob = jnp.sum(jnp.where(chosen, exps, 0.0), axis=-1, keepdims=True) / norm
        direct = jnp.sum(exps * table, axis=-1, keepdims=True) / norm
        place = lax.broadcasted_iota(jnp.int32, (1, 128), 1)
        packed = jnp.where(place == 0, reward, jnp.where(place == 1, prob, direct))
        packed = jnp.transpose(packed)
        reward, prob, direct = packed[0:1], packed[1:2], packed[2:3]
        logged_prob = propensity_ref[:, rows].astype(jnp.float32) / 65536.0
        cutoff = 0.5 * switch_ref[0].astype(jnp.float32)
        weight = jnp.minimum(prob / logged_prob, cutoff)
        rewards_ref[:, rows] = reward
        dr_ref[:, rows] = direct + weight * (logged_ref[:, rows] - reward)

    def own_block(block):
        return pl.ds(AT_OWN + block * BLOCK, BLOCK)

    for block in range(2):
        rows = hidden_ref[pl.ds(block * BLOCK, BLOCK), :].astype(jnp.float32)
        states[0, own_block(block), :] = norm_rows(rows, gain_ref[0:1, :])

    count = jnp.int32(0)
    for _, there in partners:
        count = count + jnp.where(there, 1, 0)
    pl.semaphore_wait(barrier, count)

    start_prompt(0)
    send_halo(0, 0)
    send_halo(0, 1)

    @pl.when(jnp.logical_not(has_left))
    def _():
        for layer in range(LAYERS):
            states[layer, pl.ds(AT_BEFORE, HALF), :] = jnp.zeros((HALF, width), jnp.bfloat16)

    @pl.when(jnp.logical_not(has_right))
    def _():
        for layer in range(LAYERS):
            states[layer, pl.ds(at_after, HALF), :] = jnp.zeros((HALF, width), jnp.bfloat16)

    row = lax.broadcasted_iota(jnp.int32, (BLOCK, BLOCK), 0)
    col = lax.broadcasted_iota(jnp.int32, (BLOCK, BLOCK), 1)
    for block in range(2):
        place = me * 2 + block
        off = row - col
        seen = (
            off + place * BLOCK > HALF,
            (off <= 0) & (place > 0),
            (off >= 0) & (place < 2 * n - 1),
        )
        for which, ok in enumerate(seen):
            bias_s[block, which] = jnp.where(ok, 0.0, -1e30)

    loads[0].wait()

    @pl.loop(0, tiles)
    def _(j):
        pass_on(0, j)
        project_kv(0, AT_OWN, tok_rows, j)
        project_q(0, j)

    wait_halo(0, 0)

    @pl.loop(0, tiles)
    def _(j):
        pass_on(0, j + tiles)
        project_kv(0, at_after, HALF, j)

    wait_halo(0, 1)

    @pl.loop(0, tiles)
    def _(j):
        pass_on(0, j + 2 * tiles)
        project_kv(0, AT_BEFORE, HALF, j)

    finish_passing(0, 3 * tiles)

    @pl.loop(0, tiles)
    def _(j):
        project_kv(0, AT_PROMPT, PROMPT, j)

    @pl.loop(0, pairs)
    def _(pair):
        attend(0, 0, pair)

    loads[1].wait()
    h = add_out(0, 0)
    h_s[pl.ds(0, BLOCK), :] = h
    states[1, own_block(0), :] = norm_rows(h.astype(jnp.float32), gain_ref[1:2, :])
    send_halo(1, 0)
    start_prompt(1)

    @pl.loop(0, pairs)
    def _(pair):
        pass_on(1, pair)
        attend(0, 1, pair)

    h = add_out(0, 1)
    h_s[pl.ds(BLOCK, BLOCK), :] = h
    states[1, own_block(1), :] = norm_rows(h.astype(jnp.float32), gain_ref[1:2, :])
    send_halo(1, 1)

    loads[2].wait()

    @pl.loop(0, tiles)
    def _(j):
        pass_on(1, j + pairs)
        project_kv(1, AT_OWN, tok_rows, j)
        project_q(1, j)

    wait_halo(1, 0)

    @pl.loop(0, tiles)
    def _(j):
        project_kv(1, at_after, HALF, j)

    finish_passing(1, pairs + tiles)

    @pl.loop(0, tiles)
    def _(j):
        project_kv(1, AT_PROMPT, PROMPT, j)

    @pl.loop(0, pairs)
    def _(pair):
        attend(1, 1, pair)

    loads[3].wait()
    loads[4].wait()
    head(1, add_out(1, 1))
    wait_halo(1, 1)

    @pl.loop(0, tiles)
    def _(j):
        project_kv(1, AT_BEFORE, HALF, j)

    @pl.loop(0, pairs)
    def _(pair):
        attend(1, 0, pair)

    head(0, add_out(1, 0))

    for layer in range(LAYERS):
        for side, there in ((0, has_left), (1, has_right)):

            @pl.when(there)
            def _(layer=layer, side=side):
                halo(layer, side).wait_send()

        for slot, (child, there) in enumerate(children):

            @pl.when(there)
            def _(layer=layer, slot=slot, child=child):
                for chunk in range(CHUNKS):
                    piece(layer, chunk, slot, child).wait_send()


def per_device(
    hidden_in,
    ln_gain,
    w_qkv,
    w_out,
    final_gain,
    w_heads,
    actions,
    propensity,
    logged_reward,
    switch_index,
):
    n = lax.axis_size("seq")
    tok_rows, width = hidden_in.shape
    gathered = tok_rows + 2 * HALF + PROMPT
    pairs = HEADS // 2
    vmem = pl.BlockSpec(memory_space=pltpu.VMEM)
    smem = pl.BlockSpec(memory_space=pltpu.SMEM)
    hbm = pl.BlockSpec(memory_space=pl.ANY)
    line = jax.ShapeDtypeStruct((1, tok_rows), jnp.float32)
    bf16 = jnp.bfloat16
    rewards, dr_terms = pl.pallas_call(
        functools.partial(kernel, n),
        out_shape=(line, line),
        in_specs=[vmem] * 6 + [smem] + [hbm] * 3,
        out_specs=(vmem, vmem),
        scratch_shapes=[
            pltpu.VMEM(w_qkv.shape, bf16),
            pltpu.VMEM(w_out.shape, bf16),
            pltpu.VMEM(w_heads.shape, bf16),
            pltpu.VMEM((LAYERS, gathered, width), bf16),
            pltpu.VMEM((pairs, tok_rows // BLOCK, 2 * BLOCK, PAIR), bf16),
            pltpu.VMEM((pairs, gathered, PAIR), bf16),
            pltpu.VMEM((pairs, gathered, PAIR), bf16),
            pltpu.VMEM((pairs, gathered, PAIR), bf16),
            pltpu.VMEM((BLOCK, width), bf16),
            pltpu.VMEM((tok_rows, width), bf16),
            pltpu.VMEM((tok_rows // BLOCK, 3, BLOCK, BLOCK), jnp.float32),
            pltpu.SemaphoreType.DMA((5,)),
            pltpu.SemaphoreType.DMA((LAYERS, 2)),
            pltpu.SemaphoreType.DMA((LAYERS, 2)),
            pltpu.SemaphoreType.DMA((LAYERS, 3, CHUNKS)),
            pltpu.SemaphoreType.DMA((LAYERS, CHUNKS)),
        ],
        compiler_params=pltpu.CompilerParams(
            collective_id=0, has_side_effects=True, vmem_limit_bytes=56 * 2**20
        ),
    )(
        hidden_in,
        ln_gain,
        final_gain.reshape(1, width),
        actions.reshape(1, tok_rows),
        propensity.reshape(1, tok_rows),
        logged_reward.reshape(1, tok_rows),
        switch_index,
        w_qkv,
        w_out,
        w_heads,
    )
    return rewards.reshape(tok_rows), dr_terms.reshape(tok_rows)


def solution(mesh):
    placed = (
        P(("groups", "seq"), None),
        P(),
        P(),
        P(),
        P(),
        P(),
        P(("groups", "seq")),
        P(("groups", "seq")),
        P(("groups", "seq")),
        P("groups"),
    )
    return jax.shard_map(
        per_device,
        mesh=mesh,
        in_specs=placed,
        out_specs=(P(("groups", "seq")), P(("groups", "seq"))),
        check_vma=False,
    )
```

time: 363 us -> 63.8 us (0.18)
  waiting for transfers between devices: 182 us -> 0 us
  local copies, waits for them, and re-layouts: 63.7 us -> 3.75 us
  matrix products: 57.6 us -> 0 us
  Pallas kernels: 0 us -> 57.6 us
  other arithmetic: 29.6 us -> 0 us
  between operations: 14.9 us -> 1.29 us
  starting transfers between devices: 9.11 us -> 0 us
    psum x2 -> x0, waiting for transfers between devices: 182 us -> none  [spread(): return lax.psum(block, axis)]
    dot_general x17 -> x0, matrix products: 57.6 us -> none  [the longest x4 17.9 us: attend_block(): jnp.einsum('hqk,khe->qhe', attn_probs, value_rows, preferred_element_type...]
    pallas_call x0 -> x1, Pallas kernels: none -> 57.6 us  [per_device(): pl.pallas_call(functools.partial(kernel, n), out_shape=(line, line), in_s...]
    slice x15 -> x0, local copies, waits for them, and re-layouts: 22.7 us -> none  [the longest x4 7.13 us: per_device(): band_keys = extended[:, :feat_width].reshape(-1, HEADS, HEAD)]
    reduce_sum x10 -> x0, other arithmetic: 15.3 us -> none  [the longest x4 11.4 us: attend_block(): jnp.sum(exps, axis=-1, keepdims=True)]
    select_n x4 -> x0, local copies, waits for them, and re-layouts: 14.2 us -> none  [attend_block(): jnp.where(prompt_mask[None], prompt_scores, -1e+30)]
    dynamic_slice x8 -> x0, local copies, waits for them, and re-layouts: 10.5 us -> none  [the longest x4 5.4 us: one_block(): lax.dynamic_slice_in_dim(band_values, local_start, block_rows + 2 * HALF)]
    ppermute x4 -> x0, starting transfers between devices: 8.85 us -> none  [the longest x2 5.04 us: with_halo(): before = lax.ppermute(last, axis, up)]
  transfers between devices with their start and end apart: 6 -> 0, of which waited for: 2 -> 0; matrix products, arithmetic and copies ran while one was open for 4% -> 0% of each run, Pallas kernels for 0% -> 0%
where the time goes in v1:
time: 63.8 us; the launch traced here: 62.7 us
  Pallas kernels  57.6 us (90%)
  local copies, waits for them, and re-layouts  3.75 us (6%)
  between operations  1.29 us (2%)
    pallas_call x1, Pallas kernels, per_device(): pl.pallas_call(functools.partial(kernel, n), out_shape=(line, line), in_s...  57.6 us
    unnamed x2, local copies, waits for them, and re-layouts  2.48 us
    reshape x1, local copies, waits for them, and re-layouts, per_device(): final_gain.reshape(1, width)  1.28 us

profile of v1, /device:TPU:20, one launch (start us, length us, event | category | flops | bytes accessed | tf_op | source)
XLA Modules:
  0.0 62.7 jit_solution(13536541230591436387)
XLA Ops:
  1.3 1.3 %reshape.22.final_gain_ref = f32[1,768]{1,0:T(1,128)} reshape(f32[768]{0:T(1024)} %param.14) | data formatting | bytes 6144 | tf_op jit(solution)/shard_map/reshape | solution.py:449
  2.6 57.6 %shard_map.113 = (f32[1,512]{1,0:T(1,128)}, f32[1,512]{1,0:T(1,128)}) custom-call(bf16[512,768]{1,0:T(8,128)(2,1)} %hidden_ref.1, f32[2,768]{1,0:T(2,128)} %gain_ref.1, f32[1,768]{1,0:T(1,128)} %reshape.22.final_gain_ref, s32[1,512]{1,0:T(1,128)} %bitcast.7, s32[1,512]{1,0:T(1,128)} %bitcast.8, f32[1,512]{1,0:T(1,128)} %bitcast.9, s32[1]{0:T(128)S(6)} %copy.14.switch_ref, ...), custom_call_target="tpu_custom_call" | custom-call | tf_op jit(solution)/shard_map/pallas_call | solution.py:420
  60.2 1.2 %copy.15 = f32[512]{0:T(512)} copy(f32[512]{0:T(512)} %bitcast.6) | data formatting | bytes 4096
  61.4 1.2 %copy.16 = f32[512]{0:T(512)} copy(f32[512]{0:T(512)} %bitcast.5) | data formatting | bytes 4096

commit v2 on v1

--- a/solution.py
+++ b/solution.py
@@ -17,6 +17,8 @@
 TILE = 256
 PAIR = 2 * HEAD
 CHUNKS = 4
+GROUP = 3
+BAND_GROUP = 2
 MESH = pl.DeviceIdType.MESH
 AT_PROMPT, AT_BEFORE, AT_OWN = 0, PROMPT, PROMPT + HALF
 LOG2E = 1.4426950408889634
@@ -41,8 +43,7 @@
     w_qkv_hbm,
     w_out_hbm,
     w_heads_hbm,
-    rewards_ref,
-    dr_ref,
+    out_ref,
     w_qkv,
     w_out,
     w_heads,
@@ -54,6 +55,8 @@
     att_s,
     h_s,
     bias_s,
+    part_s,
+    top_s,
     load_sem,
     halo_send,
     halo_recv,
@@ -67,12 +70,13 @@
     me = lax.axis_index("seq")
     chip, core = me // 2, me % 2
     depth = chip // 2 + chip % 2 + core
-    points = CHUNKS + (n // 2 - 1) // 2 + 2
-    parent = jnp.where(core == 1, me - 1, jnp.where(chip % 2 == 1, me - 2, me - 4))
+    points = (n // 2 - 1) // 2 + 4
+    turn = jnp.where(core == 1, points - 1, depth)
+    parent = jnp.where(core == 1, me - 1, jnp.where(chip == 1, me - 2, me - 4))
     even = core == 0
     children = (
-        (me + 4, even & (chip % 2 == 0) & (me + 4 < n)),
-        (me + 2, even & (chip % 2 == 0) & (me + 2 < n)),
+        (me + 4, even & (me + 4 < n)),
+        (me + 2, (me == 0) & (me + 2 < n)),
         (me + 1, even & (me + 1 < n)),
     )
     has_left, has_right, has_parent = me > 0, me < n - 1, me > 0
@@ -117,20 +121,20 @@
             device_id_type=MESH,
         )
 
+    def send_piece(layer, chunk):
+        for slot, (child, there) in enumerate(children):
+
+            @pl.when(there)
+            def _(slot=slot, child=child):
+                piece(layer, chunk, slot, child).start()
+
     def pass_on(layer, point):
-        chunk = point - depth
-
-        @pl.when((chunk >= 0) & (chunk < CHUNKS))
+        @pl.when(has_parent & (turn == point))
         def _():
-            @pl.when(has_parent)
-            def _():
+            @pl.loop(0, CHUNKS)
+            def _(chunk):
                 piece(layer, chunk, 0, parent).wait_recv()
-
-            for slot, (child, there) in enumerate(children):
-
-                @pl.when(there)
-                def _(slot=slot, child=child):
-                    piece(layer, chunk, slot, child).start()
+                send_piece(layer, chunk)
 
     def finish_passing(layer, done):
         if done < points:
@@ -153,6 +157,10 @@
         @pl.when(me == 0)
         def _():
             states[layer, pl.ds(AT_PROMPT, PROMPT), :] = states[layer, pl.ds(AT_OWN, PROMPT), :]
+
+            @pl.loop(0, CHUNKS)
+            def _(chunk):
+                send_piece(layer, chunk)
 
     lane = lax.broadcasted_iota(jnp.int32, (1, PAIR), 1)
     first_half = lane < HEAD
@@ -190,14 +198,13 @@
                 q_s[slot, block, pl.ds(0, BLOCK), :] = qa[rows]
                 q_s[slot, block, pl.ds(BLOCK, BLOCK), :] = qb[rows]
 
-    def attend(layer, block, pair):
+    def score(block, pair, parts):
         band = AT_BEFORE + block * BLOCK
-        starts = (AT_PROMPT, band, band + BLOCK, band + 2 * BLOCK)
-        q = q_s[pair, block]
         scores = []
-        for which, start in enumerate(starts):
+        for which in parts:
+            start = AT_PROMPT if which == 0 else band + (which - 1) * BLOCK
             s = lax.dot_general(
-                q,
+                q_s[pair, block],
                 k_s[pair, pl.ds(start, BLOCK), :],
                 (((1,), (1,)), ((), ())),
                 preferred_element_type=jnp.float32,
@@ -206,23 +213,74 @@
                 bias = bias_s[block, min(which, 2)]
                 s = jnp.concatenate([s[:BLOCK] + bias, s[BLOCK:] + bias], axis=0)
             scores.append(s)
-        top = jnp.maximum(
-            jnp.maximum(scores[0], scores[1]), jnp.maximum(scores[2], scores[3])
-        )
-        top = jnp.max(top, axis=-1, keepdims=True)
-        out_a = jnp.zeros((BLOCK, PAIR), jnp.float32)
-        out_b = jnp.zeros((BLOCK, PAIR), jnp.float32)
-        for s, start in zip(scores, starts):
-            p = jnp.exp2(s - top).astype(jnp.bfloat16)
-            out_a += jnp.dot(
+        return scores
+
+    def weigh(block, pair, parts, scores, top, out_a, out_b):
+        band = AT_BEFORE + block * BLOCK
+        for which, s in zip(parts, scores):
+            start = AT_PROMPT if which == 0 else band + (which - 1) * BLOCK
+            p = jnp.exp2((s - top).astype(jnp.bfloat16))
+            more_a = jnp.dot(
                 p[:BLOCK], va_s[pair, pl.ds(start, BLOCK), :], preferred_element_type=jnp.float32
             )
-            out_b += jnp.dot(
+            more_b = jnp.dot(
                 p[BLOCK:], vb_s[pair, pl.ds(start, BLOCK), :], preferred_element_type=jnp.float32
             )
+            out_a = more_a if out_a is None else out_a + more_a
+            out_b = more_b if out_b is None else out_b + more_b
+        return out_a, out_b
+
+    def row_top(scores):
+        return jnp.max(functools.reduce(jnp.maximum, scores), axis=-1, keepdims=True)
+
+    def finish(pair, out_a, out_b):
         total = pltpu.roll(jnp.where(first_half, out_b, out_a), HEAD, 1)
         att = jnp.where(first_half, out_a, out_b) / total
         att_s[:, pl.ds(pl.multiple_of(pair * PAIR, PAIR), PAIR)] = att.astype(jnp.bfloat16)
+
+    def in_groups(block, parts, use, size=GROUP):
+        def step(group):
+            members = [group * size + i for i in range(size)]
+            scores = score(block, members[0], parts)
+            for i, pair in enumerate(members):
+                ahead = score(block, members[i + 1], parts) if i + 1 < size else None
+                use(pair, scores)
+                scores = ahead
+
+        return step
+
+    def attend(block):
+        parts = (0, 1, 2, 3)
+
+        def use(pair, scores):
+            finish(pair, *weigh(block, pair, parts, scores, row_top(scores), None, None))
+
+        return in_groups(block, parts, use)
+
+    def attend_band(block):
+        parts = (1, 2, 3)
+
+        def use(pair, scores):
+            top = row_top(scores)
+            out_a, out_b = weigh(block, pair, parts, scores, top, None, None)
+            part_s[pair, 0] = out_a
+            part_s[pair, 1] = out_b
+            top_s[pair] = jnp.broadcast_to(top, (2 * BLOCK, PAIR))
+
+        return in_groups(block, parts, use, BAND_GROUP)
+
+    def attend_prompt(block):
+        parts = (0,)
+
+        def use(pair, scores):
+            before = top_s[pair][:, :1]
+            top = jnp.maximum(before, row_top(scores))
+            scale = jnp.exp2(before - top)
+            out_a = part_s[pair, 0] * scale[:BLOCK]
+            out_b = part_s[pair, 1] * scale[BLOCK:]
+            finish(pair, *weigh(block, pair, parts, scores, top, out_a, out_b))
+
+        return in_groups(block, parts, use)
 
     def add_out(layer, block):
         rows = pl.ds(block * BLOCK, BLOCK)
@@ -233,7 +291,7 @@
 
     def head(block, h):
         rows = pl.ds(block * BLOCK, BLOCK)
-        final = norm_rows(h.astype(jnp.float32), final_gain_ref[...])
+        final = norm_rows(h.astype(jnp.float32), final_gain_ref[...].reshape(1, width))
         out = jnp.dot(final, w_heads[...], preferred_element_type=jnp.float32)
         logits, table = out[:, :ACTIONS], out[:, ACTIONS:]
         exps = jnp.exp(logits - jnp.max(logits, axis=-1, keepdims=True))
@@ -251,8 +309,8 @@
         logged_prob = propensity_ref[:, rows].astype(jnp.float32) / 65536.0
         cutoff = 0.5 * switch_ref[0].astype(jnp.float32)
         weight = jnp.minimum(prob / logged_prob, cutoff)
-        rewards_ref[:, rows] = reward
-        dr_ref[:, rows] = direct + weight * (logged_ref[:, rows] - reward)
+        out_ref[0:1, rows] = reward
+        out_ref[1:2, rows] = direct + weight * (logged_ref[:, rows] - reward)
 
     def own_block(block):
         return pl.ds(AT_OWN + block * BLOCK, BLOCK)
@@ -297,7 +355,7 @@
 
     @pl.loop(0, tiles)
     def _(j):
-        pass_on(0, j)
+        pass_on(0, j - (tiles - 2))
         project_kv(0, AT_OWN, tok_rows, j)
         project_q(0, j)
 
@@ -305,25 +363,31 @@
 
     @pl.loop(0, tiles)
     def _(j):
-        pass_on(0, j + tiles)
         project_kv(0, at_after, HALF, j)
 
     wait_halo(0, 1)
 
     @pl.loop(0, tiles)
     def _(j):
-        pass_on(0, j + 2 * tiles)
         project_kv(0, AT_BEFORE, HALF, j)
 
-    finish_passing(0, 3 * tiles)
+    groups, band_groups = pairs // GROUP, pairs // BAND_GROUP
+    band_step, prompt_step, second_step = attend_band(0), attend_prompt(0), attend(1)
+
+    @pl.loop(0, band_groups)
+    def _(group):
+        pass_on(0, group + 2)
+        band_step(group)
+
+    finish_passing(0, 2 + band_groups)
 
     @pl.loop(0, tiles)
     def _(j):
         project_kv(0, AT_PROMPT, PROMPT, j)
 
-    @pl.loop(0, pairs)
-    def _(pair):
-        attend(0, 0, pair)
+    @pl.loop(0, groups)
+    def _(group):
+        prompt_step(group)
 
     loads[1].wait()
     h = add_out(0, 0)
@@ -332,21 +396,21 @@
     send_halo(1, 0)
     start_prompt(1)
 
-    @pl.loop(0, pairs)
-    def _(pair):
-        pass_on(1, pair)
-        attend(0, 1, pair)
+    @pl.loop(0, groups)
+    def _(group):
+        pass_on(1, group)
+        second_step(group)
 
     h = add_out(0, 1)
     h_s[pl.ds(BLOCK, BLOCK), :] = h
     states[1, own_block(1), :] = norm_rows(h.astype(jnp.float32), gain_ref[1:2, :])
     send_halo(1, 1)
 
+    pass_on(1, groups)
     loads[2].wait()
 
     @pl.loop(0, tiles)
     def _(j):
-        pass_on(1, j + pairs)
         project_kv(1, AT_OWN, tok_rows, j)
         project_q(1, j)
 
@@ -356,15 +420,22 @@
     def _(j):
         project_kv(1, at_after, HALF, j)
 
-    finish_passing(1, pairs + tiles)
+    band_step, prompt_step, first_step = attend_band(1), attend_prompt(1), attend(0)
+
+    @pl.loop(0, band_groups)
+    def _(group):
+        pass_on(1, group + groups + 1)
+        band_step(group)
+
+    finish_passing(1, groups + 1 + band_groups)
 
     @pl.loop(0, tiles)
     def _(j):
         project_kv(1, AT_PROMPT, PROMPT, j)
 
-    @pl.loop(0, pairs)
-    def _(pair):
-        attend(1, 1, pair)
+    @pl.loop(0, groups)
+    def _(group):
+        prompt_step(group)
 
     loads[3].wait()
     loads[4].wait()
@@ -375,9 +446,9 @@
     def _(j):
         project_kv(1, AT_BEFORE, HALF, j)
 
-    @pl.loop(0, pairs)
-    def _(pair):
-        attend(1, 0, pair)
+    @pl.loop(0, groups)
+    def _(group):
+        first_step(group)
 
     head(0, add_out(1, 0))
 
@@ -415,13 +486,12 @@
     vmem = pl.BlockSpec(memory_space=pltpu.VMEM)
     smem = pl.BlockSpec(memory_space=pltpu.SMEM)
     hbm = pl.BlockSpec(memory_space=pl.ANY)
-    line = jax.ShapeDtypeStruct((1, tok_rows), jnp.float32)
     bf16 = jnp.bfloat16
-    rewards, dr_terms = pl.pallas_call(
+    out = pl.pallas_call(
         functools.partial(kernel, n),
-        out_shape=(line, line),
+        out_shape=jax.ShapeDtypeStruct((2, tok_rows), jnp.float32),
         in_specs=[vmem] * 6 + [smem] + [hbm] * 3,
-        out_specs=(vmem, vmem),
+        out_specs=vmem,
         scratch_shapes=[
             pltpu.VMEM(w_qkv.shape, bf16),
             pltpu.VMEM(w_out.shape, bf16),
@@ -434,6 +504,8 @@
             pltpu.VMEM((BLOCK, width), bf16),
             pltpu.VMEM((tok_rows, width), bf16),
             pltpu.VMEM((tok_rows // BLOCK, 3, BLOCK, BLOCK), jnp.float32),
+            pltpu.VMEM((pairs, 2, BLOCK, PAIR), jnp.float32),
+            pltpu.VMEM((pairs, 2 * BLOCK, PAIR), jnp.float32),
             pltpu.SemaphoreType.DMA((5,)),
             pltpu.SemaphoreType.DMA((LAYERS, 2)),
             pltpu.SemaphoreType.DMA((LAYERS, 2)),
@@ -446,7 +518,7 @@
     )(
         hidden_in,
         ln_gain,
-        final_gain.reshape(1, width),
+        final_gain,
         actions.reshape(1, tok_rows),
         propensity.reshape(1, tok_rows),
         logged_reward.reshape(1, tok_rows),
@@ -455,7 +527,7 @@
         w_out,
         w_heads,
     )
-    return rewards.reshape(tok_rows), dr_terms.reshape(tok_rows)
+    return out[0], out[1]
 
 
 def solution(mesh):

time: 63.8 us -> 67.5 us (1.058)
  the two profiles are of different devices: /device:TPU:20 before, /device:TPU:25 now
where the time goes in v2:
time: 67.5 us; the launch traced here: 67.3 us
  Pallas kernels  64.6 us (96%)
  local copies, waits for them, and re-layouts  1.33 us (2%)
  between operations  1.29 us (2%)
    pallas_call x1, Pallas kernels, per_device(): pl.pallas_call(functools.partial(kernel, n), out_shape=jax.ShapeDtypeStru...  64.6 us

profile of v2, /device:TPU:25, one launch (start us, length us, event | category | flops | bytes accessed | tf_op | source)
XLA Modules:
  0.0 67.3 jit_solution(3846894954098245316)
XLA Ops:
  1.3 64.6 %shard_map.113 = f32[2,512]{1,0:T(2,128)} custom-call(bf16[512,768]{1,0:T(8,128)(2,1)} %hidden_ref.1, f32[2,768]{1,0:T(2,128)} %gain_ref.1, f32[768]{0:T(1024)} %final_gain_ref.1, s32[1,512]{1,0:T(1,128)} %bitcast.5, s32[1,512]{1,0:T(1,128)} %bitcast.6, f32[1,512]{1,0:T(1,128)} %bitcast.7, s32[1]{0:T(128)S(6)} %copy.12.switch_ref, ...), custom_call_target="tpu_custom_call" | custom-call | tf_op jit(solution)/shard_map/pallas_call | solution.py:490
  65.9 1.3 %fusion = (f32[1,512]{1,0:T(1,128)}, f32[1,512]{1,0:T(1,128)}) fusion(f32[2,512]{1,0:T(2,128)} %shard_map.113), kind=kLoop, calls=%fused_computation | loop fusion | bytes 8192 | tf_op jit(solution)/shard_map/slice | solution.py:530

commit v3 on v2

--- a/solution.py
+++ b/solution.py
@@ -18,7 +18,7 @@
 PAIR = 2 * HEAD
 CHUNKS = 4
 GROUP = 3
-BAND_GROUP = 2
+LOCAL_GROUP = 2
 MESH = pl.DeviceIdType.MESH
 AT_PROMPT, AT_BEFORE, AT_OWN = 0, PROMPT, PROMPT + HALF
 LOG2E = 1.4426950408889634
@@ -69,14 +69,13 @@
     pairs = HEADS // 2
     me = lax.axis_index("seq")
     chip, core = me // 2, me % 2
-    depth = chip // 2 + chip % 2 + core
-    points = (n // 2 - 1) // 2 + 4
-    turn = jnp.where(core == 1, points - 1, depth)
-    parent = jnp.where(core == 1, me - 1, jnp.where(chip == 1, me - 2, me - 4))
+    points = 2 * ((n // 2 - 1) // 2) + 2
+    turn = jnp.where(core == 1, points - 1, jnp.where(chip % 2 == 1, points - 2, chip - 1))
+    parent = jnp.where(core == 1, me - 1, jnp.where(chip % 2 == 1, me - 2, me - 4))
     even = core == 0
     children = (
-        (me + 4, even & (me + 4 < n)),
-        (me + 2, (me == 0) & (me + 2 < n)),
+        (me + 4, even & (chip % 2 == 0) & (me + 4 < n)),
+        (me + 2, even & (chip % 2 == 0) & (me + 2 < n)),
         (me + 1, even & (me + 1 < n)),
     )
     has_left, has_right, has_parent = me > 0, me < n - 1, me > 0
@@ -257,27 +256,27 @@
 
         return in_groups(block, parts, use)
 
-    def attend_band(block):
-        parts = (1, 2, 3)
+    def attend_local(block):
+        parts = (2, 3) if block == 0 else (1, 2)
 
         def use(pair, scores):
             top = row_top(scores)
             out_a, out_b = weigh(block, pair, parts, scores, top, None, None)
-            part_s[pair, 0] = out_a
-            part_s[pair, 1] = out_b
-            top_s[pair] = jnp.broadcast_to(top, (2 * BLOCK, PAIR))
-
-        return in_groups(block, parts, use, BAND_GROUP)
-
-    def attend_prompt(block):
-        parts = (0,)
+            part_s[block, pair, 0] = out_a
+            part_s[block, pair, 1] = out_b
+            top_s[block, pair] = jnp.broadcast_to(top, (2 * BLOCK, PAIR))
+
+        return in_groups(block, parts, use, LOCAL_GROUP)
+
+    def attend_rest(block):
+        parts = (0, 1) if block == 0 else (0, 3)
 
         def use(pair, scores):
-            before = top_s[pair][:, :1]
+            before = top_s[block, pair][:, :1]
             top = jnp.maximum(before, row_top(scores))
             scale = jnp.exp2(before - top)
-            out_a = part_s[pair, 0] * scale[:BLOCK]
-            out_b = part_s[pair, 1] * scale[BLOCK:]
+            out_a = part_s[block, pair, 0] * scale[:BLOCK]
+            out_b = part_s[block, pair, 1] * scale[BLOCK:]
             finish(pair, *weigh(block, pair, parts, scores, top, out_a, out_b))
 
         return in_groups(block, parts, use)
@@ -355,39 +354,41 @@
 
     @pl.loop(0, tiles)
     def _(j):
-        pass_on(0, j - (tiles - 2))
         project_kv(0, AT_OWN, tok_rows, j)
         project_q(0, j)
 
+    groups, local_groups = pairs // GROUP, pairs // LOCAL_GROUP
+    for block in range(2):
+        local_step = attend_local(block)
+
+        @pl.loop(0, local_groups)
+        def _(group, block=block, local_step=local_step):
+            pass_on(0, group + block * local_groups)
+            local_step(group)
+
+    wait_halo(0, 1)
+
+    @pl.loop(0, tiles)
+    def _(j):
+        project_kv(0, AT_BEFORE, HALF, j)
+
     wait_halo(0, 0)
 
     @pl.loop(0, tiles)
     def _(j):
         project_kv(0, at_after, HALF, j)
 
-    wait_halo(0, 1)
-
-    @pl.loop(0, tiles)
-    def _(j):
-        project_kv(0, AT_BEFORE, HALF, j)
-
-    groups, band_groups = pairs // GROUP, pairs // BAND_GROUP
-    band_step, prompt_step, second_step = attend_band(0), attend_prompt(0), attend(1)
-
-    @pl.loop(0, band_groups)
-    def _(group):
-        pass_on(0, group + 2)
-        band_step(group)
-
-    finish_passing(0, 2 + band_groups)
+    finish_passing(0, 2 * local_groups)
 
     @pl.loop(0, tiles)
     def _(j):
         project_kv(0, AT_PROMPT, PROMPT, j)
+
+    rest_first, rest_second = attend_rest(0), attend_rest(1)
 
     @pl.loop(0, groups)
     def _(group):
-        prompt_step(group)
+        rest_first(group)
 
     loads[1].wait()
     h = add_out(0, 0)
@@ -399,7 +400,7 @@
     @pl.loop(0, groups)
     def _(group):
         pass_on(1, group)
-        second_step(group)
+        rest_second(group)
 
     h = add_out(0, 1)
     h_s[pl.ds(BLOCK, BLOCK), :] = h
@@ -411,23 +412,25 @@
 
     @pl.loop(0, tiles)
     def _(j):
+        pass_on(1, j + groups + 1)
         project_kv(1, AT_OWN, tok_rows, j)
         project_q(1, j)
 
+    done = groups + 1 + tiles
+    local_step, rest_step, first_step = attend_local(1), attend_rest(1), attend(0)
+
+    @pl.loop(0, local_groups)
+    def _(group):
+        pass_on(1, jnp.where(group == 1, done, 0))
+        local_step(group)
+
     wait_halo(1, 0)
 
     @pl.loop(0, tiles)
     def _(j):
         project_kv(1, at_after, HALF, j)
 
-    band_step, prompt_step, first_step = attend_band(1), attend_prompt(1), attend(0)
-
-    @pl.loop(0, band_groups)
-    def _(group):
-        pass_on(1, group + groups + 1)
-        band_step(group)
-
-    finish_passing(1, groups + 1 + band_groups)
+    finish_passing(1, done + 1)
 
     @pl.loop(0, tiles)
     def _(j):
@@ -435,7 +438,7 @@
 
     @pl.loop(0, groups)
     def _(group):
-        prompt_step(group)
+        rest_step(group)
 
     loads[3].wait()
     loads[4].wait()
@@ -504,8 +507,8 @@
             pltpu.VMEM((BLOCK, width), bf16),
             pltpu.VMEM((tok_rows, width), bf16),
             pltpu.VMEM((tok_rows // BLOCK, 3, BLOCK, BLOCK), jnp.float32),
-            pltpu.VMEM((pairs, 2, BLOCK, PAIR), jnp.float32),
-            pltpu.VMEM((pairs, 2 * BLOCK, PAIR), jnp.float32),
+            pltpu.VMEM((tok_rows // BLOCK, pairs, 2, BLOCK, PAIR), jnp.float32),
+            pltpu.VMEM((tok_rows // BLOCK, pairs, 2 * BLOCK, PAIR), jnp.float32),
             pltpu.SemaphoreType.DMA((5,)),
             pltpu.SemaphoreType.DMA((LAYERS, 2)),
             pltpu.SemaphoreType.DMA((LAYERS, 2)),

time: 67.5 us -> 62.1 us (0.920)
  the two profiles are of different devices: /device:TPU:25 before, /device:TPU:20 now
where the time goes in v3:
time: 62.1 us; the launch traced here: 61.9 us
  Pallas kernels  59.3 us (95%)
  local copies, waits for them, and re-layouts  1.33 us (2%)
  between operations  1.29 us (2%)
    pallas_call x1, Pallas kernels, per_device(): pl.pallas_call(functools.partial(kernel, n), out_shape=jax.ShapeDtypeStru...  59.3 us
    slice x1, local copies, waits for them, and re-layouts, per_device(): return (out[0], out[1])  1.33 us

profile of v3, /device:TPU:20, one launch (start us, length us, event | category | flops | bytes accessed | tf_op | source)
XLA Modules:
  0.0 61.9 jit_solution(4031326561489490744)
XLA Ops:
  1.3 59.3 %shard_map.113 = f32[2,512]{1,0:T(2,128)} custom-call(bf16[512,768]{1,0:T(8,128)(2,1)} %hidden_ref.1, f32[2,768]{1,0:T(2,128)} %gain_ref.1, f32[768]{0:T(1024)} %final_gain_ref.1, s32[1,512]{1,0:T(1,128)} %bitcast.5, s32[1,512]{1,0:T(1,128)} %bitcast.6, f32[1,512]{1,0:T(1,128)} %bitcast.7, s32[1]{0:T(128)S(6)} %copy.12.switch_ref, ...), custom_call_target="tpu_custom_call" | custom-call | tf_op jit(solution)/shard_map/pallas_call | solution.py:493
  60.6 1.3 %fusion = (f32[1,512]{1,0:T(1,128)}, f32[1,512]{1,0:T(1,128)}) fusion(f32[2,512]{1,0:T(2,128)} %shard_map.113), kind=kLoop, calls=%fused_computation | loop fusion | bytes 8192 | tf_op jit(solution)/shard_map/slice | solution.py:533
